TPU v7x, 128 devices: a whole 4x4x4 slice. The times are simulated.
128 devices in a mesh: row: 8 (over z, core), col: 16 (over y, x).
Axes of the slice: x: 4, y: 4, z: 4, core: 2. Of those that a mesh axis runs over, the one named last changes fastest.
Arguments:
- operator: float32 [16384, 16384], P('row', 'col'), may hold values from -0.046875 to 0.046875
- vectors: float32 [16384, 256], P('row', 'col'), may hold values from -6 to 6
- owner_map: int32 [11264, 1], P(('row', 'col')), may hold values from 0 to 15; in each aligned block of 88 rows (0 to 87, 88 to 175, ...) at most 16 rows name the same one
- coupling: float32 [8, 512, 1024], P('row', 'col'), may hold values from -0.1875 to 0.1875
- ancestors: int32 [8, 16, 512], P('row', 'col'), may hold values from 0 to 1535, as said below
- leaf_modes: float32 [8, 16, 2048, 256], P('row', 'col'), may hold values from -0.375 to 0.375
- constraint_modes: float32 [8, 16, 2048, 512], P('row', 'col'), may hold values from -0.25 to 0.25
Outputs:
- separators: float32 [8, 512, 256], P('row', 'col')
- interiors: float32 [8, 16, 2048, 256], P('row', 'col')
Inputs may be any that keep to these rules, and one draw needn't show every extreme that they name: `owner_map`: in each aligned block of 88 rows no leaf is named more than 16 times, a bound that some block reaches. `ancestors`: the 512 indices of one leaf are distinct.
All inputs are finite; a program needn't handle non-finite values.
Results may differ from a plain program's by a relative error of at most 0.00007.
Values sent between devices are 32-bit elements; how exact they have to be, the bound alone decides.
A program may use at most 64 MiB of HBM per device.

v0:
```python
import jax
import jax.numpy as jnp
from jax import lax
from jax.sharding import PartitionSpec as P

highest = lax.Precision.HIGHEST


def slot_ranks(owned_rows, fanout):
    onehot = (owned_rows[..., None] == jnp.arange(fanout, dtype=jnp.int32)).astype(jnp.int32)
    running = jnp.cumsum(onehot, axis=-2)
    return jnp.sum(running * onehot, axis=-1) - 1


def on_device(operator, vectors, owner_map, coupling, ancestors, leaf_modes, constraint_modes):
    fanout = lax.axis_size("col")
    mode_local = owner_map.shape[0]
    separator_local = coupling.shape[1]
    mode_count = leaf_modes.shape[3]
    slot_count = mode_count // fanout
    mode_matrix = leaf_modes[0, 0]
    partial_adjoint = lax.dot_general(
        operator,
        lax.all_gather(vectors, "col", axis=1, tiled=True),
        (((0,), (0,)), ((), ())),
        precision=highest,
        preferred_element_type=jnp.float32,
    )
    adjoint = lax.psum(partial_adjoint, "row")
    forward = jnp.dot(operator, adjoint, precision=highest, preferred_element_type=jnp.float32)
    vector_count = forward.shape[1]
    local_rows = lax.psum_scatter(forward, "col", scatter_dimension=0, tiled=True)
    mode_rows = local_rows[:mode_local]
    separator_raw = local_rows[mode_local : mode_local + separator_local]
    top_local = local_rows[mode_local + separator_local :]
    owned_here = owner_map[:, 0]
    target = owned_here * slot_count + slot_ranks(owned_here, fanout)
    source = (
        jnp.full((fanout * slot_count,), mode_local, jnp.int32)
        .at[target]
        .set(jnp.arange(mode_local, dtype=jnp.int32))
    )
    outgoing = jnp.take(mode_rows, source, axis=0, mode="fill", fill_value=0.0).reshape(
        fanout, slot_count, vector_count
    )
    received = lax.all_to_all(outgoing, "col", split_axis=0, concat_axis=0, tiled=True)
    flattened = received.reshape(mode_count, received.shape[2])
    modal_sum = jnp.dot(
        mode_matrix, flattened, precision=highest, preferred_element_type=jnp.float32
    )
    top_gathered = lax.all_gather(top_local, ("row", "col"), axis=0, tiled=True)
    separators = separator_raw + jnp.dot(
        coupling[0], top_gathered, precision=highest, preferred_element_type=jnp.float32
    )
    separator_all = lax.all_gather(separators, "col", axis=0, tiled=True)
    candidates = jnp.concatenate([top_gathered, separator_all], axis=0)
    picked = jnp.take(candidates, ancestors[0, 0], axis=0)
    interiors = modal_sum + jnp.dot(
        constraint_modes[0, 0], picked, precision=highest, preferred_element_type=jnp.float32
    )
    return (separators[None], interiors[None, None])


def solution(mesh):
    in_specs = (
        P("row", "col"),
        P("row", "col"),
        P(("row", "col"), None),
        P("row", "col", None),
        P("row", "col", None),
        P("row", "col", None, None),
        P("row", "col", None, None),
    )
    out_specs = (P("row", "col", None), P("row", "col", None, None))
    return jax.shard_map(
        on_device, mesh=mesh, in_specs=in_specs, out_specs=out_specs, check_vma=False
    )
```

profile of v0, /device:TPU:1, one launch (start us, length us, event | category | flops | bytes accessed | tf_op | source)
XLA Modules:
  0.0 346.3 jit_solution(7148521597005728503)
XLA Ops:
  7.2 0.7 all-gather.3.cloned.1.call-update
  8.0 49.4 %all-gather.3.cloned.1.call-done = f32[2048,256]{0,1:T(8,128)} async-done(((f32[2048,16]{0,1:T(8,128)}), f32[2048,256]{0,1:T(8,128)}) %all-gather.3.cloned.1.call-update) | async-done | bytes 2097168 | tf_op jit(solution)/shard_map/all_gather | solution.py:24
  57.4 17.0 %fusion.14 = f32[1024,256]{1,0:T(8,128)} fusion(f32[2048,1024]{1,0:T(8,128)} %param.7, f32[2048,256]{0,1:T(8,128)} %all-gather.3.cloned.1.call-done), kind=kOutput, calls=%fused_computation.33 | convolution fusion | flops 6442450944 | bytes 11534336 | tf_op jit(solution)/shard_map/dot_general | solution.py:22
  74.4 0.2 reduce-scatter.2.cloned.1.call-start
  74.6 60.8 %all-reduce.2.cloned.1.call-done = f32[1024,256]{1,0:T(8,128)} async-done(((f32[1024,256]{1,0:T(8,128)}), f32[1024,256]{1,0:T(8,128)}) %all-reduce.2.cloned.1.call-update) | async-done | bytes 1048592 | tf_op jit(solution)/shard_map/psum | solution.py:29
  135.4 17.1 %convolution_bitcast_fusion = f32[2048,256]{0,1:T(8,128)} fusion(f32[1024,256]{1,0:T(8,128)} %all-reduce.2.cloned.1.call-done, f32[2048,1024]{1,0:T(8,128)} %param.7), kind=kOutput, calls=%fused_computation.7 | convolution fusion | flops 6442450944 | bytes 11534336 | tf_op jit(solution)/shard_map/dot_general | solution.py:30
  152.6 73.8 %reduce-scatter.2.cloned.1.call-done = f32[128,256]{0,1:T(8,128)} async-done(((f32[2048,256]{0,1:T(8,128)}), f32[128,256]{0,1:T(8,128)}) %reduce-scatter.2.cloned.1.call-update) | async-done | bytes 131088 | tf_op jit(solution)/shard_map/reduce_scatter | solution.py:32
  226.3 1.1 slice.17
  227.4 0.7 copy.19
  228.3 0.2 select_reduce_fusion
  228.5 0.8 scatter_custom_fusion
  229.6 1.0 copy.21
  230.5 1.0 gather_fusion
  231.5 0.8 broadcast_select_fusion
  232.3 4.4 %all-to-all-start = ((f32[16,16,256]{2,1,0:T(8,128)}), f32[16,16,256]{2,1,0:T(8,128)}, u32[]{:S(2)}, u32[]{:S(2)}) async-start(f32[16,16,256]{2,1,0:T(8,128)} %broadcast_select_fusion), calls=%async_computation.1 | async-start | bytes 524288 | tf_op jit(solution)/shard_map/all_to_all | solution.py:46
  236.8 58.2 %all-gather.5.cloned.1.call-done = f32[1024,256]{1,0:T(8,128)} async-done(((f32[8,256]{1,0:T(8,128)}), f32[1024,256]{1,0:T(8,128)}) %all-gather.5.cloned.1.call-update) | async-done | bytes 1048592 | tf_op jit(solution)/shard_map/all_gather | solution.py:51
  294.9 3.1 fusion.4
  298.1 0.7 copy.23
  298.8 16.9 %all_gather.11 = f32[512,256]{1,0:T(8,128)S(1)} all-gather(f32[32,256]{1,0:T(8,128)S(1)} %copy.22), channel_id=1, replica_groups=mesh['row'=8,'col'=16] {'col'}, dimensions={0}, use_global_device_ids=true | all-gather | bytes 557056 | tf_op jit(solution)/shard_map/all_gather | solution.py:55
  315.7 1.2 pad_maximum_fusion
  317.0 3.0 gather_fusion.1
  320.0 10.4 %fusion = f32[256,2048]{1,0:T(8,128)} fusion(f32[1,1,2048,512]{3,2,1,0:T(8,128)} %param.13, f32[512,256]{1,0:T(8,128)S(1)} %gather_fusion.1, pred[512]{0:T(512)(128)(4,1)S(1)} %compare_and_fusion), kind=kOutput, calls=%fused_computation.3 | convolution fusion | flops 3221356544 | bytes 6816256 | tf_op jit(solution)/shard_map/dot_general | solution.py:58
  330.3 6.5 %fusion.2 = f32[1,1,2048,256]{2,3,1,0:T(8,128)} fusion(f32[256,2048]{1,0:T(8,128)} %fusion, f32[256,256]{1,0:T(8,128)} %bitcast.8, f32[1,1,2048,256]{3,2,1,0:T(8,128)S(1)} %copy-done), kind=kOutput, calls=%fused_computation.6 | convolution fusion | flops 1611137024 | bytes 6553600 | tf_op jit(solution)/shard_map/dot_general | solution.py:48
  336.9 2.9 copy.24
  (31 shorter events, 0.6 us)
Async XLA Ops:
  7.2 323.2 %copy-start = (f32[1,1,2048,256]{3,2,1,0:T(8,128)S(1)}, f32[1,1,2048,256]{3,2,1,0:T(8,128)}, u32[]{:S(2)}) copy-start(f32[1,1,2048,256]{3,2,1,0:T(8,128)} %param.12) | copy-start | bytes 6291460
  7.2 50.2 %all-gather.3.cloned.1.call-start = ((), (), s32[]{:S(2)}) async-start(), calls=%async_computation.2 | async-start | bytes 2228224 | tf_op jit(solution)/shard_map/all_gather | solution.py:24
  7.9 127.5 %all-reduce.2.cloned.1.call-start = ((), (), s32[]{:S(2)}) async-start(), calls=%async_computation.3 | async-start | bytes 2097152 | tf_op jit(solution)/shard_map/psum | solution.py:29
  74.4 152.0 %reduce-scatter.2.cloned.1.call-start = ((), (), s32[]{:S(2)}) async-start(), calls=%async_computation.4 | async-start | bytes 2228224 | tf_op jit(solution)/shard_map/reduce_scatter | solution.py:32
  152.5 75.6 %copy-start.5 = (s32[88,1]{0,1:T(1,128)S(1)}, s32[88,1]{0,1:T(1,128)}, u32[]{:S(2)}) copy-start(s32[88,1]{0,1:T(1,128)} %param.9) | copy-start | bytes 1060
  152.5 77.0 %copy-start.4 = (s32[1,1,512]{2,1,0:T(1,128)S(1)}, s32[1,1,512]{2,1,0:T(1,128)}, u32[]{:S(2)}) copy-start(s32[1,1,512]{2,1,0:T(1,128)} %param.11) | copy-start | bytes 6148
  152.5 142.4 %copy-start.3 = (f32[1,32,1024]{2,1,0:T(8,128)S(1)}, f32[1,32,1024]{2,1,0:T(8,128)}, u32[]{:S(2)}) copy-start(f32[1,32,1024]{2,1,0:T(8,128)} %param.10) | copy-start | bytes 393220
  152.5 142.4 %all-gather.5.cloned.1.call-start = ((), (), s32[]{:S(2)}) async-start(), calls=%async_computation.5 | async-start | bytes 1056768 | tf_op jit(solution)/shard_map/all_gather | solution.py:51
  226.3 68.6 %copy-start.2 = (f32[128,256]{0,1:T(8,128)S(1)}, f32[128,256]{0,1:T(8,128)}, u32[]{:S(2)}) copy-start(f32[128,256]{0,1:T(8,128)} %reduce-scatter.2.cloned.1.call-done) | copy-start | bytes 393220
  232.3 98.0 %all-to-all-start = ((f32[16,16,256]{2,1,0:T(8,128)}), f32[16,16,256]{2,1,0:T(8,128)}, u32[]{:S(2)}, u32[]{:S(2)}) async-start(f32[16,16,256]{2,1,0:T(8,128)} %broadcast_select_fusion), calls=%async_computation.1 | async-start | bytes 524288 | tf_op jit(solution)/shard_map/all_to_all | solution.py:46
  294.9 20.8 %copy-start.1 = (f32[1024,256]{1,0:T(8,128)S(1)}, f32[1024,256]{1,0:T(8,128)}, u32[]{:S(2)}) copy-start(f32[1024,256]{1,0:T(8,128)} %all-gather.5.cloned.1.call-done) | copy-start | bytes 3145732
Sparse Core Ops, SparseCore 0:
  10.2 47.1 all-gather.2
  74.5 60.8 all-reduce.1
  152.6 73.6 reduce-scatter.1
  229.9 64.9 all-gather.4
where the time goes:
time: 351 us; the launch traced here: 346 us
  waiting for transfers between devices  243 us (69%)
  matrix products  54.1 us (15%)
  blocking collectives  16.9 us (5%)
  between operations  13.9 us (4%)
  local copies, waits for them, and re-layouts  11.3 us (3%)
  starting transfers between devices  4.75 us (1%)
    reduce_scatter x1, waiting for transfers between devices, on_device(): lax.psum_scatter(forward, 'col', scatter_dimension=0, tiled=True)  73.8 us
    psum x1, waiting for transfers between devices, on_device(): adjoint = lax.psum(partial_adjoint, 'row')  60.8 us
    all_gather x1, waiting for transfers between devices, on_device(): top_gathered = lax.all_gather(top_local, ('row', 'col'), axis=0, tiled=True)  58.2 us
    all_gather x1, waiting for transfers between devices, on_device(): lax.all_gather(vectors, 'col', axis=1, tiled=True)  49.4 us
    dot_general x1, matrix products, on_device(): jnp.dot(operator, adjoint, precision=highest, preferred_element_type=jnp....  17.1 us
    dot_general x1, matrix products, on_device(): lax.dot_general(operator, lax.all_gather(vectors, 'col', axis=1, tiled=Tr...  17 us
    all_gather x1, blocking collectives, on_device(): separator_all = lax.all_gather(separators, 'col', axis=0, tiled=True)  16.9 us
    dot_general x1, matrix products, on_device(): jnp.dot(constraint_modes[0, 0], picked, precision=highest, preferred_elem...  10.4 us
  transfers between devices with their start and end apart: 5, of which 4 were waited for; matrix products, arithmetic and copies ran while one was open for 7% of the time, Pallas kernels for 0%

commit v1 on v0

--- a/solution.py
+++ b/solution.py
@@ -6,10 +6,11 @@
 highest = lax.Precision.HIGHEST
 
 
-def slot_ranks(owned_rows, fanout):
-    onehot = (owned_rows[..., None] == jnp.arange(fanout, dtype=jnp.int32)).astype(jnp.int32)
-    running = jnp.cumsum(onehot, axis=-2)
-    return jnp.sum(running * onehot, axis=-1) - 1
+def slot_ranks(owned_rows):
+    rows = owned_rows.shape[0]
+    place = jnp.arange(rows, dtype=jnp.int32)
+    same = (owned_rows[:, None] == owned_rows[None, :]) & (place[None, :] < place[:, None])
+    return jnp.sum(same.astype(jnp.int32), axis=1)
 
 
 def on_device(operator, vectors, owner_map, coupling, ancestors, leaf_modes, constraint_modes):
@@ -34,7 +35,7 @@
     separator_raw = local_rows[mode_local : mode_local + separator_local]
     top_local = local_rows[mode_local + separator_local :]
     owned_here = owner_map[:, 0]
-    target = owned_here * slot_count + slot_ranks(owned_here, fanout)
+    target = owned_here * slot_count + slot_ranks(owned_here)
     source = (
         jnp.full((fanout * slot_count,), mode_local, jnp.int32)
         .at[target]

time: 351 us -> 351 us (level)
  transfers between devices with their start and end apart: 5 -> 5, of which waited for: 4 -> 4; matrix products, arithmetic and copies ran while one was open for 7% -> 6% of each run, Pallas kernels for 0% -> 0%
where the time goes in v1:
time: 351 us; the launch traced here: 346 us
  waiting for transfers between devices  243 us (69%)
  matrix products  54.1 us (15%)
  blocking collectives  16.9 us (5%)
  between operations  13.9 us (4%)
  local copies, waits for them, and re-layouts  11.3 us (3%)
  starting transfers between devices  4.75 us (1%)
    reduce_scatter x1, waiting for transfers between devices, on_device(): lax.psum_scatter(forward, 'col', scatter_dimension=0, tiled=True)  73.8 us
    psum x1, waiting for transfers between devices, on_device(): adjoint = lax.psum(partial_adjoint, 'row')  60.8 us
    all_gather x1, waiting for transfers between devices, on_device(): top_gathered = lax.all_gather(top_local, ('row', 'col'), axis=0, tiled=True)  58.4 us
    all_gather x1, waiting for transfers between devices, on_device(): lax.all_gather(vectors, 'col', axis=1, tiled=True)  49.4 us
    dot_general x1, matrix products, on_device(): jnp.dot(operator, adjoint, precision=highest, preferred_element_type=jnp....  17.1 us
    dot_general x1, matrix products, on_device(): lax.dot_general(operator, lax.all_gather(vectors, 'col', axis=1, tiled=Tr...  17 us
    all_gather x1, blocking collectives, on_device(): separator_all = lax.all_gather(separators, 'col', axis=0, tiled=True)  16.9 us
    dot_general x1, matrix products, on_device(): jnp.dot(constraint_modes[0, 0], picked, precision=highest, preferred_elem...  10.4 us
  transfers between devices with their start and end apart: 5, of which 4 were waited for; matrix products, arithmetic and copies ran while one was open for 6% of the time, Pallas kernels for 0%

profile of v1, /device:TPU:1, one launch (start us, length us, event | category | flops | bytes accessed | tf_op | source)
XLA Modules:
  0.0 346.3 jit_solution(16381814410100779000)
XLA Ops:
  7.2 0.7 all-gather.3.cloned.1.call-update
  8.0 49.4 %all-gather.3.cloned.1.call-done = f32[2048,256]{0,1:T(8,128)} async-done(((f32[2048,16]{0,1:T(8,128)}), f32[2048,256]{0,1:T(8,128)}) %all-gather.3.cloned.1.call-update) | async-done | bytes 2097168 | tf_op jit(solution)/shard_map/all_gather | solution.py:25
  57.4 17.0 %fusion.14 = f32[1024,256]{1,0:T(8,128)} fusion(f32[2048,1024]{1,0:T(8,128)} %param.7, f32[2048,256]{0,1:T(8,128)} %all-gather.3.cloned.1.call-done), kind=kOutput, calls=%fused_computation.33 | convolution fusion | flops 6442450944 | bytes 11534336 | tf_op jit(solution)/shard_map/dot_general | solution.py:23
  74.4 0.2 reduce-scatter.2.cloned.1.call-start
  74.6 60.8 %all-reduce.2.cloned.1.call-done = f32[1024,256]{1,0:T(8,128)} async-done(((f32[1024,256]{1,0:T(8,128)}), f32[1024,256]{1,0:T(8,128)}) %all-reduce.2.cloned.1.call-update) | async-done | bytes 1048592 | tf_op jit(solution)/shard_map/psum | solution.py:30
  135.4 17.1 %convolution_bitcast_fusion = f32[2048,256]{0,1:T(8,128)} fusion(f32[1024,256]{1,0:T(8,128)} %all-reduce.2.cloned.1.call-done, f32[2048,1024]{1,0:T(8,128)} %param.7), kind=kOutput, calls=%fused_computation.7 | convolution fusion | flops 6442450944 | bytes 11534336 | tf_op jit(solution)/shard_map/dot_general | solution.py:31
  152.6 73.8 %reduce-scatter.2.cloned.1.call-done = f32[128,256]{0,1:T(8,128)} async-done(((f32[2048,256]{0,1:T(8,128)}), f32[128,256]{0,1:T(8,128)}) %reduce-scatter.2.cloned.1.call-update) | async-done | bytes 131088 | tf_op jit(solution)/shard_map/reduce_scatter | solution.py:33
  226.3 1.1 slice.17
  227.4 0.7 copy.25
  228.1 0.2 convert_reduce_fusion
  228.3 0.8 scatter_custom_fusion
  229.3 1.0 copy.27
  230.3 1.0 gather_fusion
  231.3 0.8 broadcast_select_fusion
  232.1 4.4 %all-to-all-start = ((f32[16,16,256]{2,1,0:T(8,128)}), f32[16,16,256]{2,1,0:T(8,128)}, u32[]{:S(2)}, u32[]{:S(2)}) async-start(f32[16,16,256]{2,1,0:T(8,128)} %broadcast_select_fusion), calls=%async_computation.1 | async-start | bytes 524288 | tf_op jit(solution)/shard_map/all_to_all | solution.py:47
  236.5 58.4 %all-gather.5.cloned.1.call-done = f32[1024,256]{1,0:T(8,128)} async-done(((f32[8,256]{1,0:T(8,128)}), f32[1024,256]{1,0:T(8,128)}) %all-gather.5.cloned.1.call-update) | async-done | bytes 1048592 | tf_op jit(solution)/shard_map/all_gather | solution.py:52
  294.9 3.1 fusion.4
  298.1 0.7 copy.29
  298.8 16.9 %all_gather.11 = f32[512,256]{1,0:T(8,128)S(1)} all-gather(f32[32,256]{1,0:T(8,128)S(1)} %copy.28), channel_id=1, replica_groups=mesh['row'=8,'col'=16] {'col'}, dimensions={0}, use_global_device_ids=true | all-gather | bytes 557056 | tf_op jit(solution)/shard_map/all_gather | solution.py:56
  315.7 1.2 pad_maximum_fusion
  317.0 3.0 gather_fusion.1
  320.0 10.4 %fusion = f32[256,2048]{1,0:T(8,128)} fusion(f32[1,1,2048,512]{3,2,1,0:T(8,128)} %param.13, f32[512,256]{1,0:T(8,128)S(1)} %gather_fusion.1, pred[512]{0:T(512)(128)(4,1)S(1)} %compare_and_fusion), kind=kOutput, calls=%fused_computation.3 | convolution fusion | flops 3221356544 | bytes 6816256 | tf_op jit(solution)/shard_map/dot_general | solution.py:59
  330.3 6.5 %fusion.2 = f32[1,1,2048,256]{2,3,1,0:T(8,128)} fusion(f32[256,2048]{1,0:T(8,128)} %fusion, f32[256,256]{1,0:T(8,128)} %bitcast.8, f32[1,1,2048,256]{3,2,1,0:T(8,128)S(1)} %copy-done), kind=kOutput, calls=%fused_computation.6 | convolution fusion | flops 1611137024 | bytes 6553600 | tf_op jit(solution)/shard_map/dot_general | solution.py:49
  336.8 2.9 copy.30
  (29 shorter events, 0.4 us)
Async XLA Ops:
  7.2 323.2 %copy-start = (f32[1,1,2048,256]{3,2,1,0:T(8,128)S(1)}, f32[1,1,2048,256]{3,2,1,0:T(8,128)}, u32[]{:S(2)}) copy-start(f32[1,1,2048,256]{3,2,1,0:T(8,128)} %param.12) | copy-start | bytes 6291460
  7.2 50.2 %all-gather.3.cloned.1.call-start = ((), (), s32[]{:S(2)}) async-start(), calls=%async_computation.2 | async-start | bytes 2228224 | tf_op jit(solution)/shard_map/all_gather | solution.py:25
  7.9 127.5 %all-reduce.2.cloned.1.call-start = ((), (), s32[]{:S(2)}) async-start(), calls=%async_computation.3 | async-start | bytes 2097152 | tf_op jit(solution)/shard_map/psum | solution.py:30
  74.4 152.0 %reduce-scatter.2.cloned.1.call-start = ((), (), s32[]{:S(2)}) async-start(), calls=%async_computation.4 | async-start | bytes 2228224 | tf_op jit(solution)/shard_map/reduce_scatter | solution.py:33
  152.5 75.6 %copy-start.5 = (s32[88,1]{0,1:T(1,128)S(1)}, s32[88,1]{0,1:T(1,128)}, u32[]{:S(2)}) copy-start(s32[88,1]{0,1:T(1,128)} %param.9) | copy-start | bytes 1060
  152.5 76.8 %copy-start.4 = (s32[1,1,512]{2,1,0:T(1,128)S(1)}, s32[1,1,512]{2,1,0:T(1,128)}, u32[]{:S(2)}) copy-start(s32[1,1,512]{2,1,0:T(1,128)} %param.11) | copy-start | bytes 6148
  152.5 142.4 %copy-start.3 = (f32[1,32,1024]{2,1,0:T(8,128)S(1)}, f32[1,32,1024]{2,1,0:T(8,128)}, u32[]{:S(2)}) copy-start(f32[1,32,1024]{2,1,0:T(8,128)} %param.10) | copy-start | bytes 393220
  152.5 142.4 %all-gather.5.cloned.1.call-start = ((), (), s32[]{:S(2)}) async-start(), calls=%async_computation.5 | async-start | bytes 1056768 | tf_op jit(solution)/shard_map/all_gather | solution.py:52
  226.3 68.6 %copy-start.2 = (f32[128,256]{0,1:T(8,128)S(1)}, f32[128,256]{0,1:T(8,128)}, u32[]{:S(2)}) copy-start(f32[128,256]{0,1:T(8,128)} %reduce-scatter.2.cloned.1.call-done) | copy-start | bytes 393220
  232.1 98.2 %all-to-all-start = ((f32[16,16,256]{2,1,0:T(8,128)}), f32[16,16,256]{2,1,0:T(8,128)}, u32[]{:S(2)}, u32[]{:S(2)}) async-start(f32[16,16,256]{2,1,0:T(8,128)} %broadcast_select_fusion), calls=%async_computation.1 | async-start | bytes 524288 | tf_op jit(solution)/shard_map/all_to_all | solution.py:47
  294.9 20.8 %copy-start.1 = (f32[1024,256]{1,0:T(8,128)S(1)}, f32[1024,256]{1,0:T(8,128)}, u32[]{:S(2)}) copy-start(f32[1024,256]{1,0:T(8,128)} %all-gather.5.cloned.1.call-done) | copy-start | bytes 3145732
Sparse Core Ops, SparseCore 0:
  10.2 47.1 all-gather.2
  74.5 60.8 all-reduce.1
  152.6 73.6 reduce-scatter.1
  229.9 64.9 all-gather.4

commit v2 on v0

v2 whole, which is shorter than its diff:
```python
import functools

import jax
import jax.numpy as jnp
from jax import lax
from jax.experimental import pallas as pl
from jax.experimental.pallas import tpu as pltpu
from jax.sharding import PartitionSpec as P

MESH = pl.DeviceIdType.MESH
F32 = jnp.float32
BF16 = jnp.bfloat16
NH = 2
PLANE = [(dy, dx) for dy in range(4) for dx in range(4) if dy or dx]
N_REMOTE = 160


def split2(v):
    hi = v.astype(BF16)
    return hi, (v - hi.astype(F32)).astype(BF16)


def split3(v):
    hi = v.astype(BF16)
    rest = v - hi.astype(F32)
    mid = rest.astype(BF16)
    return hi, mid, (rest - mid.astype(F32)).astype(BF16)


def dot(a, b):
    return jnp.dot(a, b, preferred_element_type=F32)


def column_of(row):
    n = row.shape[1]
    eye = lax.broadcasted_iota(jnp.int32, (n, n), 0) == lax.broadcasted_iota(jnp.int32, (n, n), 1)
    return jnp.sum(jnp.where(eye, jnp.broadcast_to(row, (n, n)), 0.0), axis=1, keepdims=True)


def kernel(
    op_hbm, x_hbm, owner_ref, coup_ref, anc_ref, lm_hbm, cm_hbm,
    sep_out, int_hbm,
    k32, lm32, cm32, kh, kl, lmh, lml, cmh, cml,
    xg, xl, part, core_in, zsum, z_in, at, w, f,
    ra1, ra2, ra3, ra4, rb1, rb2, rb3, rb4,
    loc, own, orow, gsel, outgo, coordin, top, candt, sepall, inter,
    ss, rs, ls,
):
    row, col = lax.axis_index("row"), lax.axis_index("col")
    z, core, y, x = row // 2, row % 2, col // 4, col % 4

    def dev(dz=0, dc=0, dy=0, dx=0):
        return (((z + dz) % 4) * 2 + (core + dc) % 2, ((y + dy) % 4) * 4 + (x + dx) % 4)

    copies = []

    def send(src, dst, where):
        i = len(copies)
        c = pltpu.make_async_remote_copy(
            src_ref=src, dst_ref=dst, send_sem=ss.at[i], recv_sem=rs.at[i], device_id=where, device_id_type=MESH
        )
        c.start()
        copies.append(c)
        return c

    xp, xm, yp, ym = dev(dx=1), dev(dx=3), dev(dy=1), dev(dy=3)
    mate = dev(dc=1)

    loads = []

    def load(src, dst):
        c = pltpu.make_async_copy(src, dst, ls.at[len(loads)])
        c.start()
        loads.append(c)
        return c

    x_loads = [load(x_hbm.at[pl.ds(8 * h, 8)], xg.at[h, 0, 0]) for h in range(NH)]
    k_loads = [load(op_hbm.at[pl.ds(256 * i, 256)], k32.at[pl.ds(256 * i, 256)]) for i in range(8)]
    cm_load = load(cm_hbm, cm32)
    lm_load = load(lm_hbm, lm32)

    barrier = pltpu.get_barrier_semaphore()
    friends = [dev(dy=dy, dx=dx) for dy, dx in PLANE] + [dev(dz=d) for d in (1, 2, 3)] + [mate]
    for d in friends:
        pl.semaphore_signal(barrier, inc=1, device_id=d, device_id_type=MESH)
    pl.semaphore_wait(barrier, len(friends))
    for c in x_loads:
        c.wait()

    A, B = pl.ds(0, 1024), pl.ds(1024, 1024)
    A0, A1, B0, B1 = pl.ds(0, 512), pl.ds(512, 512), pl.ds(1024, 512), pl.ds(1536, 512)
    ag = [dict() for _ in range(NH)]

    def own_sends(h):
        s = xg.at[h, 0, 0]
        ag[h]["xp"] = send(s, xg.at[h, 0, 3], xp)
        ag[h]["xm"] = send(s, xg.at[h, 0, 1], xm)
        ag[h]["yp"] = send(s, xg.at[h, 3, 0], yp)
        ag[h]["ym"] = send(s, xg.at[h, 1, 0], ym)

    def to_y(h, dx):
        s = xg.at[h, 0, dx, :, A]
        return [send(s, xg.at[h, 3, dx, :, A], yp), send(s, xg.at[h, 1, dx, :, A], ym)]

    def to_x(h, dy):
        s = xg.at[h, dy, 0, :, B]
        return [send(s, xg.at[h, dy, 3, :, B], xp), send(s, xg.at[h, dy, 1, :, B], xm)]

    def step2(h):
        a = ag[h]
        a["xp"].wait_recv()
        a["fa"] = [send(xg.at[h, 0, 3, :, A0], xg.at[h, 0, 2, :, A0], xp)]
        a["yp"].wait_recv()
        a["fb"] = [send(xg.at[h, 3, 0, :, B0], xg.at[h, 2, 0, :, B0], yp)]
        a["xm"].wait_recv()
        a["fa"].append(send(xg.at[h, 0, 1, :, A1], xg.at[h, 0, 2, :, A1], xm))
        a["ym"].wait_recv()
        a["fb"].append(send(xg.at[h, 1, 0, :, B1], xg.at[h, 2, 0, :, B1], ym))
        a["ta"] = to_y(h, 3)
        a["tb"] = to_x(h, 3)
        a["ta"] += to_y(h, 1)
        a["tb"] += to_x(h, 1)

    def step3(h):
        a = ag[h]
        for c in a["fa"]:
            c.wait_recv()
        a["ta"] += to_y(h, 2)
        for c in a["fb"]:
            c.wait_recv()
        a["tb"] += to_x(h, 2)

    def step4(h):
        a = ag[h]
        for c in a["ta"]:
            c.wait_recv()
        a["end"] = [
            send(xg.at[h, 3, :, :, A0], xg.at[h, 2, :, :, A0], yp),
            send(xg.at[h, 1, :, :, A1], xg.at[h, 2, :, :, A1], ym),
        ]
        for c in a["tb"]:
            c.wait_recv()
        a["end"] += [
            send(xg.at[h, :, 3, :, B0], xg.at[h, :, 2, :, B0], xp),
            send(xg.at[h, :, 1, :, B1], xg.at[h, :, 2, :, B1], xm),
        ]

    def step5(h):
        for c in ag[h]["end"]:
            c.wait_recv()
        for q in range(8):
            rows = []
            for j in (2 * q, 2 * q + 1):
                rows.append(xg[h, (j // 4 + 4 - y) % 4, (j % 4 + 4 - x) % 4])
            hi, lo = split2(jnp.concatenate(rows, axis=0))
            xl[h, pl.ds(16 * q, 16), :] = hi
            xl[h, pl.ds(128 + 16 * q, 16), :] = lo

    def split_k(i):
        k_loads[i].wait()

        @pl.loop(0, 8)
        def _(j):
            r = pl.ds(pl.multiple_of(256 * i + 32 * j, 32), 32)
            hi, lo = split2(k32[r, :])
            kh[r, :] = hi
            kl[r, :] = lo

    def mm1(h, n):
        c = pl.ds(256 * n, 256)
        p = dot(xl[h], kh[:, c])
        p = p[:128] + p[128:] + dot(xl[h, 0:128], kl[:, c])
        part[h, :, :, :, c] = p.reshape(2, 4, 16, 256)

    ar = [dict() for _ in range(NH)]

    def ar1(h):
        ar[h]["c"] = send(part.at[h, 1 - core], core_in.at[h], mate)

    def ar2(h):
        ar[h]["c"].wait_recv()
        zsum[h] = part[h, core] + core_in[h]
        ar[h]["z"] = [send(zsum.at[h, (z + d) % 4], z_in.at[h, d - 1], dev(dz=d)) for d in (2, 1, 3)]

    def ar3(h):
        for c in ar[h]["z"]:
            c.wait_recv()
        at[h, core, z] = zsum[h, z] + z_in[h, 0] + z_in[h, 1] + z_in[h, 2]
        s = at.at[h, core, z]
        ar[h]["g"] = [(d, send(s, s, dev(dz=d))) for d in (2, 1, 3)]
        ar[h]["m"] = [send(s, s, mate)]

    def ar4(h):
        for d, c in sorted(ar[h]["g"], key=lambda t: t[0] % 2 == 0):
            c.wait_recv()
            s = at.at[h, core, (z + 4 - d) % 4]
            ar[h]["m"].append(send(s, s, mate))

    def ar5(h):
        for c in ar[h]["m"]:
            c.wait_recv()
        for n in range(8):
            c = pl.ds(128 * n, 128)
            hi, lo = split2(at[h, :, :, :, c].reshape(128, 128).T)
            w[h, c, 0:128] = hi
            w[h, c, 128:256] = lo

    def mm2(h, slots):
        for dy, dx in slots:
            b = ((y + dy) % 4) * 4 + (x + dx) % 4
            r = pl.ds(pl.multiple_of(b * 128, 128), 128)
            p = dot(kh[r, :], w[h])
            f[h, dy, dx] = p[:, :128] + p[:, 128:] + dot(kl[r, :], w[h, :, 0:128])

    rc = [dict() for _ in range(NH)]
    lo32, hi32, lo64 = pl.ds(0, 32), pl.ds(32, 32), pl.ds(0, 64)
    lo32b, hi32b, hi64 = pl.ds(64, 32), pl.ds(96, 32), pl.ds(64, 64)

    def rs1(h):
        mm2(h, [(dy, 2) for dy in range(4)])
        rc[h]["a1"] = [
            send(f.at[h, :, 2, lo32], ra1.at[h, 0], xp),
            send(f.at[h, :, 2, hi32], ra1.at[h, 1], xm),
        ]
        mm2(h, [(2, dx) for dx in (0, 1, 3)])
        rc[h]["b1"] = [
            send(f.at[h, 2, :, lo32b], rb1.at[h, 0], yp),
            send(f.at[h, 2, :, hi32b], rb1.at[h, 1], ym),
        ]
        mm2(h, [(1, 1), (3, 1), (0, 1), (1, 3), (3, 3), (0, 3), (1, 0), (3, 0), (0, 0)])

    def rs2(h):
        for c in rc[h]["a1"]:
            c.wait_recv()
        f[h, :, 1, 0:32] += ra1[h, 0]
        f[h, :, 3, 32:64] += ra1[h, 1]
        rc[h]["a2"] = [
            send(f.at[h, :, 1, lo64], ra2.at[h, 0], xp),
            send(f.at[h, :, 3, lo64], ra2.at[h, 1], xm),
        ]
        for c in rc[h]["b1"]:
            c.wait_recv()
        f[h, 1, :, 64:96] += rb1[h, 0]
        f[h, 3, :, 96:128] += rb1[h, 1]
        rc[h]["b2"] = [
            send(f.at[h, 1, :, hi64], rb2.at[h, 0], yp),
            send(f.at[h, 3, :, hi64], rb2.at[h, 1], ym),
        ]

    def rs3(h):
        for c in rc[h]["a2"]:
            c.wait_recv()
        f[h, :, 0, 0:64] += ra2[h, 0] + ra2[h, 1]
        rc[h]["a3"] = [
            send(f.at[h, 2, 0, lo32], ra3.at[h, 0], yp),
            send(f.at[h, 2, 0, hi32], ra3.at[h, 1], ym),
        ]
        for c in rc[h]["b2"]:
            c.wait_recv()
        f[h, 0, :, 64:128] += rb2[h, 0] + rb2[h, 1]
        rc[h]["b3"] = [
            send(f.at[h, 0, 2, lo32b], rb3.at[h, 0], xp),
            send(f.at[h, 0, 2, hi32b], rb3.at[h, 1], xm),
        ]

    def rs4(h):
        for c in rc[h]["a3"]:
            c.wait_recv()
        f[h, 1, 0, 0:32] += ra3[h, 0]
        f[h, 3, 0, 32:64] += ra3[h, 1]
        rc[h]["a4"] = [
            send(f.at[h, 1, 0, lo64], ra4.at[h, 0], yp),
            send(f.at[h, 3, 0, lo64], ra4.at[h, 1], ym),
        ]
        for c in rc[h]["b3"]:
            c.wait_recv()
        f[h, 0, 1, 64:96] += rb3[h, 0]
        f[h, 0, 3, 96:128] += rb3[h, 1]
        rc[h]["b4"] = [
            send(f.at[h, 0, 1, hi64], rb4.at[h, 0], xp),
            send(f.at[h, 0, 3, hi64], rb4.at[h, 1], xm),
        ]

    def rs5(h):
        for c in rc[h]["a4"] + rc[h]["b4"]:
            c.wait_recv()
        c = pl.ds(128 * h, 128)
        loc[0:64, c] = f[h, 0, 0, 0:64] + ra4[h, 0] + ra4[h, 1]
        loc[64:128, c] = f[h, 0, 0, 64:128] + rb4[h, 0] + rb4[h, 1]

    def select_modes():
        orow[...] = jnp.full((1, 128), -1.0, F32)
        orow[:, 0:88] = owner_ref[...].astype(F32)
        r = orow[...]
        c = column_of(r)
        q, p = lax.broadcasted_iota(jnp.int32, (128, 128), 0), lax.broadcasted_iota(jnp.int32, (128, 128), 1)
        rank = jnp.sum(jnp.where((c == r) & (q < p), 1.0, 0.0), axis=0, keepdims=True)
        target = jnp.where(r < 0.0, -1.0, r * 16.0 + rank)
        slot = lax.broadcasted_iota(jnp.int32, (256, 128), 0).astype(F32)
        own[...] = jnp.where(slot == target, 1.0, 0.0).astype(BF16)

    def select_ancestors():
        for i in range(4):
            c = column_of(anc_ref[:, pl.ds(128 * i, 128)].astype(F32))
            for j in range(3):
                place = lax.broadcasted_iota(jnp.int32, (128, 512), 1).astype(F32) + 512.0 * j
                gsel[pl.ds(128 * i, 128), pl.ds(512 * j, 512)] = jnp.where(c == place, 1.0, 0.0).astype(BF16)

    def split_rows(src, hi_ref, lo_ref, rows):
        @pl.loop(0, 2048 // rows)
        def _(j):
            r = pl.ds(pl.multiple_of(rows * j, rows), rows)
            hi, lo = split2(src[r, :])
            hi_ref[r, :] = hi
            lo_ref[r, :] = lo

    own_sends(0)
    own_sends(1)
    split_k(0)
    split_k(1)
    step2(0)
    split_k(2)
    step2(1)
    split_k(3)
    step3(0)
    split_k(4)
    step3(1)
    split_k(5)
    step4(0)
    split_k(6)
    split_k(7)
    step5(0)
    mm1(0, 0)
    mm1(0, 1)
    step4(1)
    mm1(0, 2)
    mm1(0, 3)
    ar1(0)
    step5(1)
    ar2(0)
    mm1(1, 0)
    mm1(1, 1)
    mm1(1, 2)
    mm1(1, 3)
    ar1(1)
    ar3(0)
    ar2(1)
    select_modes()
    select_ancestors()
    ar4(0)
    ar5(0)
    ar3(1)
    rs1(0)
    ar4(1)
    rs2(0)
    ar5(1)
    rs3(0)
    rs1(1)
    rs4(0)
    rs2(1)
    rs5(0)
    cm_load.wait()
    split_rows(cm32, cmh, cml, 32)
    rs3(1)
    lm_load.wait()
    split_rows(lm32, lmh, lml, 64)
    rs4(1)
    rs5(1)

    pv, pp = lax.broadcasted_iota(jnp.int32, (256, 256), 1), lax.broadcasted_iota(jnp.int32, (256, 256), 0)
    order = jnp.where(pp == ((pv // 8) % 2) * 128 + (pv // 16) * 8 + pv % 8, 1.0, 0.0).astype(BF16)
    a, b, c = split3(loc[...])
    mine = dot(a, order) + dot(b, order) + dot(c, order)

    top[z, core, col] = mine[120:128]
    s = top.at[z, core, col]
    tz = [send(s, s, dev(dz=d)) for d in (2, 1, 3)]

    hi, lo = split2(mine)
    out = dot(own[...], hi) + dot(own[...], lo)
    outgo[...] = out.reshape(16, 16, 256)
    coordin[col] = outgo[col]

    for t in tz:
        t.wait_recv()
    s = top.at[:, core, col]
    tp = [send(s, s, dev(dy=dy, dx=dx)) for dy, dx in PLANE]
    mx = []
    for dy, dx in PLANE:
        d = dev(dy=dy, dx=dx)
        mx.append(send(outgo.at[d[1]], coordin.at[col], d))
    ch, cl = split2(coup_ref[...])
    cc = jnp.concatenate([ch, cl], axis=0)
    for t in tp:
        t.wait_recv()
    s = top.at[:, core]
    tc = send(s, s, mate)
    tc.wait_recv()
    hi, lo = split2(top[...].reshape(1024, 256))
    candt[:, 0:256] = hi
    candt[:, 256:512] = lo
    p = dot(cc, hi)
    sep = mine[88:120] + (p[:32] + p[32:] + dot(ch, lo))
    sep_out[...] = sep
    sepall[col] = sep
    s = sepall.at[col]
    se = [send(s, s, dev(dy=dy, dx=dx)) for dy, dx in PLANE]
    gath = dot(gsel[:, 0:1024], candt[...])
    for t in mx:
        t.wait_recv()
    hi, lo = split2(coordin[...].reshape(256, 256))
    for i in range(4):
        r = pl.ds(512 * i, 512)
        inter[r, :] = dot(lmh[r, :], hi) + dot(lmh[r, :], lo) + dot(lml[r, :], hi)
    for t in se:
        t.wait_recv()
    hi, lo = split2(sepall[...].reshape(512, 256))
    gath = gath + dot(gsel[:, 1024:1536], jnp.concatenate([hi, lo], axis=1))
    hi, lo = gath[:, :256].astype(BF16), gath[:, 256:].astype(BF16)
    outs = []
    for i in range(4):
        r = pl.ds(512 * i, 512)
        inter[r, :] += dot(cmh[r, :], hi) + dot(cmh[r, :], lo) + dot(cml[r, :], hi)
        outs.append(load(inter.at[r], int_hbm.at[r]))
    for t in outs:
        t.wait()
    for t in copies:
        t.wait_send()


def on_device(operator, vectors, owner_map, coupling, ancestors, leaf_modes, constraint_modes):
    vmem, anywhere = pl.BlockSpec(memory_space=pltpu.VMEM), pl.BlockSpec(memory_space=pl.ANY)
    scratch = [
        ((2048, 1024), F32), ((2048, 256), F32), ((2048, 512), F32),
        ((2048, 1024), BF16), ((2048, 1024), BF16),
        ((2048, 256), BF16), ((2048, 256), BF16), ((2048, 512), BF16), ((2048, 512), BF16),
        ((NH, 4, 4, 8, 2048), F32), ((NH, 256, 2048), BF16),
        ((NH, 2, 4, 16, 1024), F32), ((NH, 4, 16, 1024), F32),
        ((NH, 4, 16, 1024), F32), ((NH, 3, 16, 1024), F32), ((NH, 2, 4, 16, 1024), F32),
        ((NH, 1024, 256), BF16), ((NH, 4, 4, 128, 128), F32),
        ((NH, 2, 4, 32, 128), F32), ((NH, 2, 4, 64, 128), F32), ((NH, 2, 32, 128), F32), ((NH, 2, 64, 128), F32),
        ((NH, 2, 4, 32, 128), F32), ((NH, 2, 4, 64, 128), F32), ((NH, 2, 32, 128), F32), ((NH, 2, 64, 128), F32),
        ((128, 256), F32), ((256, 128), BF16), ((1, 128), F32), ((512, 1536), BF16),
        ((16, 16, 256), F32), ((16, 16, 256), F32), ((4, 2, 16, 8, 256), F32),
        ((1024, 512), BF16), ((16, 32, 256), F32), ((2048, 256), F32),
    ]
    separators, interiors = pl.pallas_call(
        kernel,
        out_shape=(jax.ShapeDtypeStruct((32, 256), F32), jax.ShapeDtypeStruct((2048, 256), F32)),
        in_specs=[anywhere, anywhere, vmem, vmem, vmem, anywhere, anywhere],
        out_specs=(vmem, anywhere),
        scratch_shapes=[pltpu.VMEM(s, t) for s, t in scratch]
        + [pltpu.SemaphoreType.DMA((N_REMOTE,)), pltpu.SemaphoreType.DMA((N_REMOTE,)), pltpu.SemaphoreType.DMA((16,))],
        compiler_params=pltpu.CompilerParams(collective_id=0, has_side_effects=True, vmem_limit_bytes=61 << 20),
        cost_estimate=pl.CostEstimate(flops=9_000_000_000, bytes_accessed=20_000_000, transcendentals=0),
        name="step",
    )(
        operator, vectors.T, owner_map.reshape(1, 88), coupling[0], ancestors[0],
        leaf_modes[0, 0], constraint_modes[0, 0],
    )
    return separators[None], interiors[None, None]


def solution(mesh):
    in_specs = (
        P("row", "col"),
        P("row", "col"),
        P(("row", "col"), None),
        P("row", "col", None),
        P("row", "col", None),
        P("row", "col", None, None),
        P("row", "col", None, None),
    )
    out_specs = (P("row", "col", None), P("row", "col", None, None))
    return jax.shard_map(
        on_device, mesh=mesh, in_specs=in_specs, out_specs=out_specs, check_vma=False
    )
```

time: 351 us -> 103 us (0.29); the launches traced: 346 us -> 103 us
  waiting for transfers between devices: 243 us -> 0 us
  Pallas kernels: 0 us -> 97.5 us
  matrix products: 54.1 us -> 0 us
  blocking collectives: 16.9 us -> 0 us
  between operations: 13.9 us -> 0.64 us
  local copies, waits for them, and re-layouts: 11.3 us -> 4.42 us
  starting transfers between devices: 4.75 us -> 0 us
    all_gather x2 -> x0, waiting for transfers between devices: 108 us -> none  [the longest x1 58.2 us: on_device(): top_gathered = lax.all_gather(top_local, ('row', 'col'), axis=0, tiled=True)]
    pallas_call x0 -> x1, Pallas kernels: none -> 97.5 us  [on_device(): pl.pallas_call(kernel, out_shape=(jax.ShapeDtypeStruct((32, 256), F32), j...]
    reduce_scatter x1 -> x0, waiting for transfers between devices: 73.8 us -> none  [on_device(): lax.psum_scatter(forward, 'col', scatter_dimension=0, tiled=True)]
    psum x1 -> x0, waiting for transfers between devices: 60.8 us -> none  [on_device(): adjoint = lax.psum(partial_adjoint, 'row')]
    dot_general x5 -> x0, matrix products: 54.1 us -> none  [the longest x1 17.1 us: on_device(): jnp.dot(operator, adjoint, precision=highest, preferred_element_type=jnp....]
    all_gather x1 -> x0, blocking collectives: 16.9 us -> none  [on_device(): separator_all = lax.all_gather(separators, 'col', axis=0, tiled=True)]
    all_to_all x1 -> x0, starting transfers between devices: 4.41 us -> none  [on_device(): lax.all_to_all(outgoing, 'col', split_axis=0, concat_axis=0, tiled=True)]
    gather x2 -> x0, local copies, waits for them, and re-layouts: 3.94 us -> none  [the longest x1 2.97 us: on_device(): picked = jnp.take(candidates, ancestors[0, 0], axis=0)]
  transfers between devices with their start and end apart: 5 -> 0, of which waited for: 4 -> 0; matrix products, arithmetic and copies ran while one was open for 7% -> 0% of each run, Pallas kernels for 0% -> 0%
where the time goes in v2:
time: 103 us
  Pallas kernels  97.5 us (95%)
  local copies, waits for them, and re-layouts  4.42 us (4%)
    pallas_call x1, Pallas kernels, on_device(): pl.pallas_call(kernel, out_shape=(jax.ShapeDtypeStruct((32, 256), F32), j...  97.5 us
    unnamed x2, local copies, waits for them, and re-layouts  4.42 us

profile of v2, /device:TPU:1, one launch (start us, length us, event | category | flops | bytes accessed | tf_op | source)
XLA Modules:
  0.0 102.6 jit_solution(2949075811304804334)
XLA Ops:
  0.6 97.5 %step.1 = (f32[32,256]{1,0:T(8,128)}, f32[2048,256]{1,0:T(8,128)}) custom-call(f32[2048,1024]{1,0:T(8,128)} %op_hbm.1, f32[16,2048]{1,0:T(8,128)} %bitcast.12, s32[1,88]{1,0:T(1,128)} %bitcast.15, f32[32,1024]{1,0:T(8,128)} %bitcast.13, s32[1,512]{1,0:T(1,128)} %bitcast.14, f32[2048,256]{1,0:T(8,128)} %bitcast.11, f32[2048,512]{1,0:T(8,128)} %bitcast.10), custom_call_target="tpu_custom_call" | custom-call | flops 8999999488 | bytes 20000000 | tf_op jit(solution)/shard_map/step/pallas_call | solution.py:447
  98.2 1.4 %copy.11 = f32[1,32,256]{2,1,0:T(8,128)} copy(f32[1,32,256]{2,1,0:T(8,128)} %bitcast.9) | data formatting | bytes 65536
  99.5 3.0 %copy.12 = f32[1,1,2048,256]{3,2,1,0:T(8,128)} copy(f32[1,1,2048,256]{3,2,1,0:T(8,128)} %bitcast.8) | data formatting | bytes 4194304

commit v3 on v2

v3 whole, which is shorter than its diff:
```python
import functools

import jax
import jax.numpy as jnp
from jax import lax
from jax.experimental import pallas as pl
from jax.experimental.pallas import tpu as pltpu
from jax.sharding import PartitionSpec as P

MESH = pl.DeviceIdType.MESH
F32 = jnp.float32
BF16 = jnp.bfloat16
NH = 2
PLANE = [(dy, dx) for dy in range(4) for dx in range(4) if dy or dx]
N_REMOTE = 200
STOP = None
FAR_FIRST = sorted(PLANE, key=lambda p: -min(p[0], 4 - p[0]) - min(p[1], 4 - p[1]))
VMEM_STEP = 57 << 20


def split2(v):
    hi = v.astype(BF16)
    return hi, (v - hi.astype(F32)).astype(BF16)


def split3(v):
    hi = v.astype(BF16)
    rest = v - hi.astype(F32)
    mid = rest.astype(BF16)
    return hi, mid, (rest - mid.astype(F32)).astype(BF16)


def dot(a, b):
    return jnp.dot(a, b, preferred_element_type=F32)


def column_of(row):
    n = row.shape[1]
    eye = lax.broadcasted_iota(jnp.int32, (n, n), 0) == lax.broadcasted_iota(jnp.int32, (n, n), 1)
    return jnp.sum(jnp.where(eye, jnp.broadcast_to(row, (n, n)), 0.0), axis=1, keepdims=True)


class Sent:
    def __init__(self, copy):
        self.copy, self.landed = copy, False

    def wait_recv(self):
        if not self.landed:
            self.copy.wait_recv()
        self.landed = True


class Loaded:
    def __init__(self, copy):
        self.copy, self.landed = copy, False

    def wait(self):
        if not self.landed:
            self.copy.wait()
        self.landed = True


def kernel(
    op_hbm, x_hbm, owner_ref, coup_ref, anc_ref,
    sep_out, gath_out, coord_out,
    k32, kh, kl, xg, xl, part, core_in, zsum, z_in, at, w, f,
    ra1, ra2, ra3, rb1, rb2, rb3,
    loc, own, orow, gsel, outgo, coordin, top, cc, sepall,
    ss, rs, ls,
):
    row, col = lax.axis_index("row"), lax.axis_index("col")
    z, core, y, x = row // 2, row % 2, col // 4, col % 4

    def dev(dz=0, dc=0, dy=0, dx=0):
        return (((z + dz) % 4) * 2 + (core + dc) % 2, ((y + dy) % 4) * 4 + (x + dx) % 4)

    copies = []

    def send(src, dst, where):
        i = len(copies)
        c = pltpu.make_async_remote_copy(
            src_ref=src, dst_ref=dst, send_sem=ss.at[i], recv_sem=rs.at[i], device_id=where, device_id_type=MESH
        )
        c.start()
        copies.append(Sent(c))
        return copies[-1]

    xp, xm, yp, ym = dev(dx=1), dev(dx=3), dev(dy=1), dev(dy=3)
    mate = dev(dc=1)

    loads = []

    def load(src, dst):
        c = pltpu.make_async_copy(src, dst, ls.at[len(loads)])
        c.start()
        loads.append(Loaded(c))
        return loads[-1]

    x_loads = [load(x_hbm.at[pl.ds(8 * h, 8)], xg.at[h, 0, 0]) for h in range(NH)]
    k_loads = [load(op_hbm.at[pl.ds(256 * i, 256)], k32.at[pl.ds(256 * i, 256)]) for i in range(8)]
    barrier = pltpu.get_barrier_semaphore()
    friends = [dev(dy=dy, dx=dx) for dy, dx in PLANE] + [dev(dz=d) for d in (1, 2, 3)] + [mate]
    for d in friends:
        pl.semaphore_signal(barrier, inc=1, device_id=d, device_id_type=MESH)
    pl.semaphore_wait(barrier, len(friends))
    for c in x_loads:
        c.wait()

    A, B = pl.ds(0, 1024), pl.ds(1024, 1024)
    A0, A1, B0, B1 = pl.ds(0, 512), pl.ds(512, 512), pl.ds(1024, 512), pl.ds(1536, 512)
    ag = [dict() for _ in range(NH)]

    def own_sends(h):
        s, a = xg.at[h, 0, 0], ag[h]
        a["xp"] = send(s, xg.at[h, 0, 3], xp)
        a["xm"] = send(s, xg.at[h, 0, 1], xm)
        a["yp"] = send(s, xg.at[h, 3, 0], yp)
        a["ym"] = send(s, xg.at[h, 1, 0], ym)
        a["xo"] = send(xg.at[h, 0, 0, :, A], xg.at[h, 0, 2, :, A], dev(dx=2))
        a["yo"] = send(xg.at[h, 0, 0, :, B], xg.at[h, 2, 0, :, B], dev(dy=2))

    def to_y(h, dx):
        s = xg.at[h, 0, dx, :, A]
        return [send(s, xg.at[h, 3, dx, :, A], yp), send(s, xg.at[h, 1, dx, :, A], ym)]

    def to_x(h, dy):
        s = xg.at[h, dy, 0, :, B]
        return [send(s, xg.at[h, dy, 3, :, B], xp), send(s, xg.at[h, dy, 1, :, B], xm)]

    def step2(h):
        a = ag[h]
        a["ta"], a["tb"] = [], []
        a["xp"].wait_recv()
        a["ta"] += to_y(h, 3)
        a["yp"].wait_recv()
        a["tb"] += to_x(h, 3)
        a["xm"].wait_recv()
        a["ta"] += to_y(h, 1)
        a["ym"].wait_recv()
        a["tb"] += to_x(h, 1)

    def step3(h):
        a = ag[h]
        a["xo"].wait_recv()
        a["ta"] += to_y(h, 2)
        a["yo"].wait_recv()
        a["tb"] += to_x(h, 2)

    def step4(h):
        a = ag[h]
        for c in a["ta"]:
            c.wait_recv()
        a["end"] = [
            send(xg.at[h, 3, :, :, A0], xg.at[h, 2, :, :, A0], yp),
            send(xg.at[h, 1, :, :, A1], xg.at[h, 2, :, :, A1], ym),
        ]
        for c in a["tb"]:
            c.wait_recv()
        a["end"] += [
            send(xg.at[h, :, 3, :, B0], xg.at[h, :, 2, :, B0], xp),
            send(xg.at[h, :, 1, :, B1], xg.at[h, :, 2, :, B1], xm),
        ]

    def step5(h):
        for c in ag[h]["end"]:
            c.wait_recv()
        for q in range(8):
            rows = []
            for j in (2 * q, 2 * q + 1):
                rows.append(xg[h, (j // 4 + 4 - y) % 4, (j % 4 + 4 - x) % 4])
            hi, lo = split2(jnp.concatenate(rows, axis=0))
            xl[h, pl.ds(16 * q, 16), :] = hi
            xl[h, pl.ds(128 + 16 * q, 16), :] = lo

    def split_k(i):
        k_loads[i].wait()

        @pl.loop(0, 8)
        def _(j):
            r = pl.ds(pl.multiple_of(256 * i + 32 * j, 32), 32)
            hi, lo = split2(k32[r, :])
            kh[r, :] = hi
            kl[r, :] = lo

    def mm1(h, n):
        c = pl.ds(256 * n, 256)
        p = dot(xl[h], kh[:, c])
        p = p[:128] + p[128:] + dot(xl[h, 0:128], kl[:, c])
        part[h, :, :, :, c] = p.reshape(2, 4, 16, 256)

    ar = [dict() for _ in range(NH)]

    def ar1(h):
        ar[h]["c"] = send(part.at[h, 1 - core], core_in.at[h], mate)

    def ar2(h):
        ar[h]["c"].wait_recv()
        zsum[h] = part[h, core] + core_in[h]
        ar[h]["z"] = [send(zsum.at[h, (z + d) % 4], z_in.at[h, d - 1], dev(dz=d)) for d in (2, 1, 3)]

    def ar3(h):
        for c in ar[h]["z"]:
            c.wait_recv()
        at[h, core, z] = zsum[h, z] + z_in[h, 0] + z_in[h, 1] + z_in[h, 2]
        s = at.at[h, core, z]
        ar[h]["g"] = [(d, send(s, s, dev(dz=d))) for d in (2, 1, 3)]
        ar[h]["m"] = [send(s, s, mate)]

    def ar4(h):
        for d, c in sorted(ar[h]["g"], key=lambda t: t[0] % 2 == 0):
            c.wait_recv()
            s = at.at[h, core, (z + 4 - d) % 4]
            ar[h]["m"].append(send(s, s, mate))

    def ar5(h):
        for c in ar[h]["m"]:
            c.wait_recv()
        for n in range(8):
            c = pl.ds(128 * n, 128)
            hi, lo = split2(at[h, :, :, :, c].reshape(128, 128).T)
            w[h, c, 0:128] = hi
            w[h, c, 128:256] = lo

    def mm2(h, slots):
        for dy, dx in slots:
            b = ((y + dy) % 4) * 4 + (x + dx) % 4
            r = pl.ds(pl.multiple_of(b * 128, 128), 128)
            p = dot(kh[r, :], w[h])
            f[h, dy, dx] = p[:, :128] + p[:, 128:] + dot(kl[r, :], w[h, :, 0:128])

    rc = [dict() for _ in range(NH)]
    lo32, hi32, lo64 = pl.ds(0, 32), pl.ds(32, 32), pl.ds(0, 64)
    lo32b, hi32b, hi64 = pl.ds(64, 32), pl.ds(96, 32), pl.ds(64, 64)

    def rs1(h):
        mm2(h, [(dy, 2) for dy in range(4)])
        rc[h]["a1"] = [
            send(f.at[h, :, 2, lo32], ra1.at[h, 0], xp),
            send(f.at[h, :, 2, hi32], ra1.at[h, 1], xm),
        ]
        mm2(h, [(2, dx) for dx in (0, 1, 3)])
        rc[h]["b1"] = [
            send(f.at[h, 2, :, lo32b], rb1.at[h, 0], yp),
            send(f.at[h, 2, :, hi32b], rb1.at[h, 1], ym),
        ]
        mm2(h, [(1, 1), (3, 1), (0, 1), (1, 3), (3, 3), (0, 3), (1, 0), (3, 0), (0, 0)])

    def rs2(h):
        for c in rc[h]["a1"]:
            c.wait_recv()
        f[h, :, 1, 0:32] += ra1[h, 0]
        f[h, :, 3, 32:64] += ra1[h, 1]
        rc[h]["a2"] = [
            send(f.at[h, :, 1, lo64], ra2.at[h, 0], xp),
            send(f.at[h, :, 3, lo64], ra2.at[h, 1], xm),
        ]
        for c in rc[h]["b1"]:
            c.wait_recv()
        f[h, 1, :, 64:96] += rb1[h, 0]
        f[h, 3, :, 96:128] += rb1[h, 1]
        rc[h]["b2"] = [
            send(f.at[h, 1, :, hi64], rb2.at[h, 0], yp),
            send(f.at[h, 3, :, hi64], rb2.at[h, 1], ym),
        ]

    def rs3(h):
        for c in rc[h]["a2"]:
            c.wait_recv()
        f[h, :, 0, 0:64] += ra2[h, 0] + ra2[h, 1]
        rc[h]["a3"] = [send(f.at[h, d, 0, lo64], ra3.at[h, d - 1], dev(dy=d)) for d in (2, 1, 3)]
        for c in rc[h]["b2"]:
            c.wait_recv()
        f[h, 0, :, 64:128] += rb2[h, 0] + rb2[h, 1]
        rc[h]["b3"] = [send(f.at[h, 0, d, hi64], rb3.at[h, d - 1], dev(dx=d)) for d in (2, 1, 3)]

    def rs5(h):
        for c in rc[h]["b3"]:
            c.wait_recv()
        loc[h, 64:128] = f[h, 0, 0, 64:128] + rb3[h, 0] + rb3[h, 1] + rb3[h, 2]

    def rs6(h):
        for c in rc[h]["a3"]:
            c.wait_recv()
        loc[h, 0:64] = f[h, 0, 0, 0:64] + ra3[h, 0] + ra3[h, 1] + ra3[h, 2]

    def select_modes():
        orow[...] = jnp.full((1, 128), -1.0, F32)
        orow[:, 0:88] = owner_ref[...].astype(F32)
        r = orow[...]
        c = column_of(r)
        q, p = lax.broadcasted_iota(jnp.int32, (128, 128), 0), lax.broadcasted_iota(jnp.int32, (128, 128), 1)
        rank = jnp.sum(jnp.where((c == r) & (q < p), 1.0, 0.0), axis=0, keepdims=True)
        target = jnp.where(r < 0.0, -1.0, r * 16.0 + rank)
        slot = lax.broadcasted_iota(jnp.int32, (256, 128), 0).astype(F32)
        own[...] = jnp.where(slot == target, 1.0, 0.0).astype(BF16)

    def select_ancestors():
        for i in range(4):
            c = column_of(anc_ref[:, pl.ds(128 * i, 128)].astype(F32))
            for j in range(3):
                place = lax.broadcasted_iota(jnp.int32, (128, 512), 1).astype(F32) + 512.0 * j
                gsel[pl.ds(128 * i, 128), pl.ds(512 * j, 512)] = jnp.where(c == place, 1.0, 0.0).astype(BF16)

    t = [dict() for _ in range(NH)]

    def top_z(h):
        top[h, z, core, col] = loc[h, 120:128]
        s = top.at[h, z, core, col]
        t[h]["tz"] = [send(s, s, dev(dz=d)) for d in (2, 1, 3)]

    def top_plane(h):
        for c in t[h]["tz"]:
            c.wait_recv()
        s = top.at[h, :, core, col]
        t[h]["tp"] = [send(s, s, dev(dy=dy, dx=dx)) for dy, dx in FAR_FIRST]

    def mode_send(h):
        hi, lo = split2(loc[h])
        out = dot(own[...], jnp.concatenate([hi, lo], axis=1))
        outgo[h] = (out[:, :128] + out[:, 128:]).reshape(16, 16, 128)
        coordin[h, col] = outgo[h, col]
        t[h]["mx"] = []
        for dy, dx in FAR_FIRST:
            d = dev(dy=dy, dx=dx)
            t[h]["mx"].append(send(outgo.at[h, d[1]], coordin.at[h, col], d))

    def top_core(h):
        for c in t[h]["tp"]:
            c.wait_recv()
        s = top.at[h, :, core]
        t[h]["tc"] = send(s, s, mate)

    def split_coupling():
        ch, cl = split2(coup_ref[...])
        cc[0:32, :] = ch
        cc[32:64, :] = cl

    def separators(h):
        t[h]["tc"].wait_recv()
        hi, lo = split2(top[h].reshape(1024, 128))
        c = jnp.concatenate([hi, lo], axis=1)
        p = dot(cc[...], c)
        sep = loc[h, 88:120] + (p[:32, :128] + p[:32, 128:] + p[32:, :128])
        sep_out[h] = sep
        sepall[h, col] = sep
        s = sepall.at[h, col]
        t[h]["se"] = [send(s, s, dev(dy=dy, dx=dx)) for dy, dx in FAR_FIRST]
        t[h]["cand"] = c

    def gather_top(h):
        t[h]["gath"] = dot(gsel[:, 0:1024], t[h]["cand"])

    def mode_recv(h):
        for c in t[h]["mx"]:
            c.wait_recv()
        coord_out[h] = coordin[h].reshape(256, 128)

    def gather_sep(h):
        for c in t[h]["se"]:
            c.wait_recv()
        hi, lo = split2(sepall[h].reshape(512, 128))
        gath = t[h]["gath"] + dot(gsel[:, 1024:1536], jnp.concatenate([hi, lo], axis=1))
        gath_out[h] = gath.astype(BF16)

    def sent():
        for c in copies:
            c.wait_recv()
            c.copy.wait_send()
        for c in loads:
            c.wait()

    program = [
        (own_sends, 0), (own_sends, 1), (select_modes,), (select_ancestors,), (split_coupling,),
        (step2, 0), (step3, 0), (split_k, 0), (split_k, 1), (split_k, 2), (split_k, 3), (step2, 1), (step3, 1),
        (split_k, 4), (split_k, 5), (split_k, 6), (split_k, 7), (step4, 0), (step4, 1), (step5, 0),
        (mm1, 0, 0), (mm1, 0, 1), (mm1, 0, 2), (mm1, 0, 3), (ar1, 0), (ar2, 0), (step5, 1),
        (mm1, 1, 0), (mm1, 1, 1), (mm1, 1, 2), (mm1, 1, 3), (ar1, 1), (ar2, 1), (ar3, 0),
        (ar4, 0), (ar3, 1), (ar5, 0), (rs1, 0), (ar4, 1), (rs2, 0), (ar5, 1), (rs1, 1), (rs3, 0), (rs2, 1),
        (rs5, 0), (top_z, 0), (rs6, 0), (rs3, 1), (top_plane, 0), (mode_send, 0), (rs5, 1), (top_z, 1), (rs6, 1),
        (top_plane, 1), (top_core, 0), (mode_send, 1), (separators, 0), (top_core, 1), (gather_top, 0),
        (separators, 1), (gather_top, 1), (gather_sep, 0), (mode_recv, 0), (mode_recv, 1), (gather_sep, 1),
    ]
    for step, *args in program[:STOP] + [(sent,)]:
        step(*args)


def last(cm_ref, lm_ref, sep_ref, gath_ref, coord_ref, sep_out, int_out, gh, gl, ch, cl):
    @pl.when(pl.program_id(0) == 0)
    def _():
        pv, pp = lax.broadcasted_iota(jnp.int32, (256, 256), 1), lax.broadcasted_iota(jnp.int32, (256, 256), 0)
        order = jnp.where(pp == ((pv // 8) % 2) * 128 + (pv // 16) * 8 + pv % 8, 1.0, 0.0).astype(BF16)
        a, b, c = split3(jnp.concatenate([sep_ref[0], sep_ref[1]], axis=1))
        sep_out[...] = dot(a, order) + dot(b, order) + dot(c, order)
        gh[...] = dot(jnp.concatenate([gath_ref[0, :, 0:128], gath_ref[1, :, 0:128]], axis=1), order).astype(BF16)
        gl[...] = dot(jnp.concatenate([gath_ref[0, :, 128:256], gath_ref[1, :, 128:256]], axis=1), order).astype(BF16)
        a, b = split2(jnp.concatenate([coord_ref[0], coord_ref[1]], axis=1))
        ch[...] = dot(a, order).astype(BF16)
        cl[...] = dot(b, order).astype(BF16)

    mh, ml = split2(cm_ref[...])
    total = dot(mh, gh[...]) + dot(mh, gl[...]) + dot(ml, gh[...])
    mh, ml = split2(lm_ref[...])
    int_out[...] = total + (dot(mh, ch[...]) + dot(mh, cl[...]) + dot(ml, ch[...]))


def on_device(operator, vectors, owner_map, coupling, ancestors, leaf_modes, constraint_modes):
    vmem, anywhere = pl.BlockSpec(memory_space=pltpu.VMEM), pl.BlockSpec(memory_space=pl.ANY)
    scratch = [
        ((2048, 1024), F32), ((2048, 1024), BF16), ((2048, 1024), BF16),
        ((NH, 4, 4, 8, 2048), F32), ((NH, 256, 2048), BF16),
        ((NH, 2, 4, 16, 1024), F32), ((NH, 4, 16, 1024), F32),
        ((NH, 4, 16, 1024), F32), ((NH, 3, 16, 1024), F32), ((NH, 2, 4, 16, 1024), F32),
        ((NH, 1024, 256), BF16), ((NH, 4, 4, 128, 128), F32),
        ((NH, 2, 4, 32, 128), F32), ((NH, 2, 4, 64, 128), F32), ((NH, 3, 64, 128), F32),
        ((NH, 2, 4, 32, 128), F32), ((NH, 2, 4, 64, 128), F32), ((NH, 3, 64, 128), F32),
        ((NH, 128, 128), F32), ((256, 128), BF16), ((1, 128), F32), ((512, 1536), BF16),
        ((NH, 16, 16, 128), F32), ((NH, 16, 16, 128), F32), ((NH, 4, 2, 16, 8, 128), F32),
        ((64, 1024), BF16), ((NH, 16, 32, 128), F32),
    ]
    sep, gath, coords = pl.pallas_call(
        kernel,
        out_shape=(
            jax.ShapeDtypeStruct((NH, 32, 128), F32),
            jax.ShapeDtypeStruct((NH, 512, 256), BF16),
            jax.ShapeDtypeStruct((NH, 256, 128), F32),
        ),
        in_specs=[anywhere, anywhere, vmem, vmem, vmem],
        out_specs=(vmem, vmem, vmem),
        scratch_shapes=[pltpu.VMEM(s, t) for s, t in scratch]
        + [pltpu.SemaphoreType.DMA((N_REMOTE,)), pltpu.SemaphoreType.DMA((N_REMOTE,)), pltpu.SemaphoreType.DMA((16,))],
        compiler_params=pltpu.CompilerParams(collective_id=0, has_side_effects=True, vmem_limit_bytes=VMEM_STEP),
        cost_estimate=pl.CostEstimate(flops=9_000_000_000, bytes_accessed=20_000_000, transcendentals=0),
        name="step",
    )(operator, vectors.T, owner_map.reshape(1, 88), coupling[0], ancestors[0])

    def whole(*shape):
        return pl.BlockSpec(shape, lambda i: (0,) * len(shape))

    def rows(width):
        return pl.BlockSpec((512, width), lambda i: (i, 0))

    separators, interiors = pl.pallas_call(
        last,
        grid=(4,),
        out_shape=(jax.ShapeDtypeStruct((32, 256), F32), jax.ShapeDtypeStruct((2048, 256), F32)),
        in_specs=[rows(512), rows(256), whole(NH, 32, 128), whole(NH, 512, 256), whole(NH, 256, 128)],
        out_specs=(whole(32, 256), rows(256)),
        scratch_shapes=[pltpu.VMEM(s, BF16) for s in ((512, 256), (512, 256), (256, 256), (256, 256))],
        compiler_params=pltpu.CompilerParams(vmem_limit_bytes=57 << 20),
        name="last",
    )(constraint_modes[0, 0], leaf_modes[0, 0], sep, gath, coords)
    return separators[None], interiors[None, None]


def solution(mesh):
    in_specs = (
        P("row", "col"),
        P("row", "col"),
        P(("row", "col"), None),
        P("row", "col", None),
        P("row", "col", None),
        P("row", "col", None, None),
        P("row", "col", None, None),
    )
    out_specs = (P("row", "col", None), P("row", "col", None, None))
    return jax.shard_map(
        on_device, mesh=mesh, in_specs=in_specs, out_specs=out_specs, check_vma=False
    )
```

time: 103 us -> 88.5 us (0.86)
  Pallas kernels: 97.5 us -> 87.7 us
  local copies, waits for them, and re-layouts: 4.42 us -> 0 us
    pallas_call x1 -> x2, Pallas kernels: 97.5 us -> 87.7 us  [the longest x1 80.7 us: on_device(): pl.pallas_call(kernel, out_shape=(jax.ShapeDtypeStruct((NH, 32, 128), F32...]
    unnamed x2 -> x0, local copies, waits for them, and re-layouts: 4.42 us -> none
where the time goes in v3:
time: 88.5 us; the launch traced here: 88.3 us
  Pallas kernels  87.7 us (99%)
    pallas_call x1, Pallas kernels, on_device(): pl.pallas_call(kernel, out_shape=(jax.ShapeDtypeStruct((NH, 32, 128), F32...  80.7 us
    pallas_call x1, Pallas kernels, on_device(): pl.pallas_call(last, grid=(4,), out_shape=(jax.ShapeDtypeStruct((32, 256)...  6.92 us

profile of v3, /device:TPU:1, one launch (start us, length us, event | category | flops | bytes accessed | tf_op | source)
XLA Modules:
  0.0 88.3 jit_solution(4271174746196495400)
XLA Ops:
  0.6 80.7 %step.1 = (f32[2,32,128]{2,1,0:T(8,128)}, bf16[2,512,256]{2,1,0:T(8,128)(2,1)}, f32[2,256,128]{2,1,0:T(8,128)}) custom-call(f32[2048,1024]{1,0:T(8,128)} %op_hbm.1, f32[16,2048]{1,0:T(8,128)} %bitcast.11, s32[1,88]{1,0:T(1,128)} %bitcast.15, f32[32,1024]{1,0:T(8,128)} %bitcast.12, s32[1,512]{1,0:T(1,128)} %bitcast.14), custom_call_target="tpu_custom_call" | custom-call | flops 8999999488 | bytes 20000000 | tf_op jit(solution)/shard_map/step/pallas_call | solution.py:420
  81.4 6.9 %last.1 = (f32[32,256]{1,0:T(8,128)}, f32[2048,256]{1,0:T(8,128)}) custom-call(f32[2048,512]{1,0:T(8,128)} %bitcast.8, f32[2048,256]{1,0:T(8,128)} %bitcast.9, f32[2,32,128]{2,1,0:T(8,128)} %get-tuple-element.7.sep_ref, bf16[2,512,256]{2,1,0:T(8,128)(2,1)} %get-tuple-element.8.gath_ref, f32[2,256,128]{2,1,0:T(8,128)} %get-tuple-element.9.coord_ref), custom_call_target="tpu_custom_call" | custom-call | tf_op jit(solution)/shard_map/last/pallas_call | solution.py:442

commit v4 on v3

--- a/solution.py
+++ b/solution.py
@@ -42,7 +42,7 @@
 
 class Sent:
     def __init__(self, copy):
-        self.copy, self.landed = copy, False
+        self.copy, self.landed, self.left = copy, False, False
 
     def wait_recv(self):
         if not self.landed:
@@ -61,11 +61,11 @@
 
 
 def kernel(
-    op_hbm, x_hbm, owner_ref, coup_ref, anc_ref,
+    op_hbm, x_hbm, owner_hbm, coup_hbm, anc_hbm,
     sep_out, gath_out, coord_out,
     k32, kh, kl, xg, xl, part, core_in, zsum, z_in, at, w, f,
-    ra1, ra2, ra3, rb1, rb2, rb3,
-    loc, own, orow, gsel, outgo, coordin, top, cc, sepall,
+    ra2, ra3, rb2, rb3,
+    owner_ref, anc_ref, coup_ref, loc, own, orow, gsel, outgo, coordin, top, cc, sepall,
     ss, rs, ls,
 ):
     row, col = lax.axis_index("row"), lax.axis_index("col")
@@ -98,6 +98,8 @@
 
     x_loads = [load(x_hbm.at[pl.ds(8 * h, 8)], xg.at[h, 0, 0]) for h in range(NH)]
     k_loads = [load(op_hbm.at[pl.ds(256 * i, 256)], k32.at[pl.ds(256 * i, 256)]) for i in range(8)]
+    i_loads = [load(owner_hbm, owner_ref), load(anc_hbm, anc_ref), load(coup_hbm, coup_ref)]
+
     barrier = pltpu.get_barrier_semaphore()
     friends = [dev(dy=dy, dx=dx) for dy, dx in PLANE] + [dev(dz=d) for d in (1, 2, 3)] + [mate]
     for d in friends:
@@ -229,48 +231,38 @@
             f[h, dy, dx] = p[:, :128] + p[:, 128:] + dot(kl[r, :], w[h, :, 0:128])
 
     rc = [dict() for _ in range(NH)]
-    lo32, hi32, lo64 = pl.ds(0, 32), pl.ds(32, 32), pl.ds(0, 64)
-    lo32b, hi32b, hi64 = pl.ds(64, 32), pl.ds(96, 32), pl.ds(64, 64)
+    lo64, hi64 = pl.ds(0, 64), pl.ds(64, 64)
+
+    def to_rows(h, dx):
+        rc[h]["a2"].append(send(f.at[h, :, dx, lo64], ra2.at[h, dx - 1], dev(dx=dx)))
+
+    def to_columns(h, dy):
+        rc[h]["b2"].append(send(f.at[h, dy, :, hi64], rb2.at[h, dy - 1], dev(dy=dy)))
 
     def rs1(h):
+        rc[h]["a2"], rc[h]["b2"] = [], []
         mm2(h, [(dy, 2) for dy in range(4)])
-        rc[h]["a1"] = [
-            send(f.at[h, :, 2, lo32], ra1.at[h, 0], xp),
-            send(f.at[h, :, 2, hi32], ra1.at[h, 1], xm),
-        ]
+        to_rows(h, 2)
         mm2(h, [(2, dx) for dx in (0, 1, 3)])
-        rc[h]["b1"] = [
-            send(f.at[h, 2, :, lo32b], rb1.at[h, 0], yp),
-            send(f.at[h, 2, :, hi32b], rb1.at[h, 1], ym),
-        ]
-        mm2(h, [(1, 1), (3, 1), (0, 1), (1, 3), (3, 3), (0, 3), (1, 0), (3, 0), (0, 0)])
-
-    def rs2(h):
-        for c in rc[h]["a1"]:
-            c.wait_recv()
-        f[h, :, 1, 0:32] += ra1[h, 0]
-        f[h, :, 3, 32:64] += ra1[h, 1]
-        rc[h]["a2"] = [
-            send(f.at[h, :, 1, lo64], ra2.at[h, 0], xp),
-            send(f.at[h, :, 3, lo64], ra2.at[h, 1], xm),
-        ]
-        for c in rc[h]["b1"]:
-            c.wait_recv()
-        f[h, 1, :, 64:96] += rb1[h, 0]
-        f[h, 3, :, 96:128] += rb1[h, 1]
-        rc[h]["b2"] = [
-            send(f.at[h, 1, :, hi64], rb2.at[h, 0], yp),
-            send(f.at[h, 3, :, hi64], rb2.at[h, 1], ym),
-        ]
+        to_columns(h, 2)
+        mm2(h, [(0, 1), (1, 1), (3, 1)])
+        to_rows(h, 1)
+        mm2(h, [(1, 0), (1, 3)])
+        to_columns(h, 1)
+        mm2(h, [(0, 3), (3, 3)])
+        to_rows(h, 3)
+        mm2(h, [(3, 0)])
+        to_columns(h, 3)
+        mm2(h, [(0, 0)])
 
     def rs3(h):
         for c in rc[h]["a2"]:
             c.wait_recv()
-        f[h, :, 0, 0:64] += ra2[h, 0] + ra2[h, 1]
+        f[h, :, 0, 0:64] += ra2[h, 0] + ra2[h, 1] + ra2[h, 2]
         rc[h]["a3"] = [send(f.at[h, d, 0, lo64], ra3.at[h, d - 1], dev(dy=d)) for d in (2, 1, 3)]
         for c in rc[h]["b2"]:
             c.wait_recv()
-        f[h, 0, :, 64:128] += rb2[h, 0] + rb2[h, 1]
+        f[h, 0, :, 64:128] += rb2[h, 0] + rb2[h, 1] + rb2[h, 2]
         rc[h]["b3"] = [send(f.at[h, 0, d, hi64], rb3.at[h, d - 1], dev(dx=d)) for d in (2, 1, 3)]
 
     def rs5(h):
@@ -284,6 +276,8 @@
         loc[h, 0:64] = f[h, 0, 0, 0:64] + ra3[h, 0] + ra3[h, 1] + ra3[h, 2]
 
     def select_modes():
+        for c in i_loads:
+            c.wait()
         orow[...] = jnp.full((1, 128), -1.0, F32)
         orow[:, 0:88] = owner_ref[...].astype(F32)
         r = orow[...]
@@ -362,10 +356,16 @@
         gath = t[h]["gath"] + dot(gsel[:, 1024:1536], jnp.concatenate([hi, lo], axis=1))
         gath_out[h] = gath.astype(BF16)
 
+    def settle():
+        for c in copies:
+            if c.landed and not c.left:
+                c.copy.wait_send()
+                c.left = True
+
     def sent():
         for c in copies:
             c.wait_recv()
-            c.copy.wait_send()
+        settle()
         for c in loads:
             c.wait()
 
@@ -375,10 +375,10 @@
         (split_k, 4), (split_k, 5), (split_k, 6), (split_k, 7), (step4, 0), (step4, 1), (step5, 0),
         (mm1, 0, 0), (mm1, 0, 1), (mm1, 0, 2), (mm1, 0, 3), (ar1, 0), (ar2, 0), (step5, 1),
         (mm1, 1, 0), (mm1, 1, 1), (mm1, 1, 2), (mm1, 1, 3), (ar1, 1), (ar2, 1), (ar3, 0),
-        (ar4, 0), (ar3, 1), (ar5, 0), (rs1, 0), (ar4, 1), (rs2, 0), (ar5, 1), (rs1, 1), (rs3, 0), (rs2, 1),
+        (settle,), (ar4, 0), (ar3, 1), (ar5, 0), (rs1, 0), (ar4, 1), (ar5, 1), (rs1, 1), (settle,), (rs3, 0),
         (rs5, 0), (top_z, 0), (rs6, 0), (rs3, 1), (top_plane, 0), (mode_send, 0), (rs5, 1), (top_z, 1), (rs6, 1),
-        (top_plane, 1), (top_core, 0), (mode_send, 1), (separators, 0), (top_core, 1), (gather_top, 0),
-        (separators, 1), (gather_top, 1), (gather_sep, 0), (mode_recv, 0), (mode_recv, 1), (gather_sep, 1),
+        (settle,), (top_plane, 1), (top_core, 0), (mode_send, 1), (separators, 0), (settle,), (top_core, 1), (gather_top, 0),
+        (separators, 1), (gather_top, 1), (settle,), (gather_sep, 0), (mode_recv, 0), (mode_recv, 1), (settle,), (gather_sep, 1),
     ]
     for step, *args in program[:STOP] + [(sent,)]:
         step(*args)
@@ -411,8 +411,9 @@
         ((NH, 2, 4, 16, 1024), F32), ((NH, 4, 16, 1024), F32),
         ((NH, 4, 16, 1024), F32), ((NH, 3, 16, 1024), F32), ((NH, 2, 4, 16, 1024), F32),
         ((NH, 1024, 256), BF16), ((NH, 4, 4, 128, 128), F32),
-        ((NH, 2, 4, 32, 128), F32), ((NH, 2, 4, 64, 128), F32), ((NH, 3, 64, 128), F32),
-        ((NH, 2, 4, 32, 128), F32), ((NH, 2, 4, 64, 128), F32), ((NH, 3, 64, 128), F32),
+        ((NH, 3, 4, 64, 128), F32), ((NH, 3, 64, 128), F32),
+        ((NH, 3, 4, 64, 128), F32), ((NH, 3, 64, 128), F32),
+        ((1, 88), jnp.int32), ((1, 512), jnp.int32), ((32, 1024), F32),
         ((NH, 128, 128), F32), ((256, 128), BF16), ((1, 128), F32), ((512, 1536), BF16),
         ((NH, 16, 16, 128), F32), ((NH, 16, 16, 128), F32), ((NH, 4, 2, 16, 8, 128), F32),
         ((64, 1024), BF16), ((NH, 16, 32, 128), F32),
@@ -424,7 +425,7 @@
             jax.ShapeDtypeStruct((NH, 512, 256), BF16),
             jax.ShapeDtypeStruct((NH, 256, 128), F32),
         ),
-        in_specs=[anywhere, anywhere, vmem, vmem, vmem],
+        in_specs=[anywhere] * 5,
         out_specs=(vmem, vmem, vmem),
         scratch_shapes=[pltpu.VMEM(s, t) for s, t in scratch]
         + [pltpu.SemaphoreType.DMA((N_REMOTE,)), pltpu.SemaphoreType.DMA((N_REMOTE,)), pltpu.SemaphoreType.DMA((16,))],
@@ -437,11 +438,11 @@
         return pl.BlockSpec(shape, lambda i: (0,) * len(shape))
 
     def rows(width):
-        return pl.BlockSpec((512, width), lambda i: (i, 0))
+        return pl.BlockSpec((1024, width), lambda i: (i, 0))
 
     separators, interiors = pl.pallas_call(
         last,
-        grid=(4,),
+        grid=(2,),
         out_shape=(jax.ShapeDtypeStruct((32, 256), F32), jax.ShapeDtypeStruct((2048, 256), F32)),
         in_specs=[rows(512), rows(256), whole(NH, 32, 128), whole(NH, 512, 256), whole(NH, 256, 128)],
         out_specs=(whole(32, 256), rows(256)),

time: 88.5 us -> 85.5 us (0.966)
  Pallas kernels: 87.7 us -> 84.8 us
    pallas_call x1, Pallas kernels: 80.7 us -> 78.5 us  [on_device(): pl.pallas_call(kernel, out_shape=(jax.ShapeDtypeStruct((NH, 32, 128), F32...]
where the time goes in v4:
time: 85.5 us; the launch traced here: 85.4 us
  Pallas kernels  84.8 us (99%)
    pallas_call x1, Pallas kernels, on_device(): pl.pallas_call(kernel, out_shape=(jax.ShapeDtypeStruct((NH, 32, 128), F32...  78.5 us
    pallas_call x1, Pallas kernels, on_device(): pl.pallas_call(last, grid=(2,), out_shape=(jax.ShapeDtypeStruct((32, 256)...  6.32 us

profile of v4, /device:TPU:1, one launch (start us, length us, event | category | flops | bytes accessed | tf_op | source)
XLA Modules:
  0.0 85.4 jit_solution(15526547276331628045)
XLA Ops:
  0.6 78.5 %step.1 = (f32[2,32,128]{2,1,0:T(8,128)}, bf16[2,512,256]{2,1,0:T(8,128)(2,1)}, f32[2,256,128]{2,1,0:T(8,128)}) custom-call(f32[2048,1024]{1,0:T(8,128)} %op_hbm.1, f32[16,2048]{1,0:T(8,128)} %bitcast.11, s32[1,88]{1,0:T(1,128)} %bitcast.15, f32[32,1024]{1,0:T(8,128)} %bitcast.12, s32[1,512]{1,0:T(1,128)} %bitcast.14), custom_call_target="tpu_custom_call" | custom-call | flops 8999999488 | bytes 20000000 | tf_op jit(solution)/shard_map/step/pallas_call | solution.py:421
  79.1 6.3 %last.1 = (f32[32,256]{1,0:T(8,128)}, f32[2048,256]{1,0:T(8,128)}) custom-call(f32[2048,512]{1,0:T(8,128)} %bitcast.8, f32[2048,256]{1,0:T(8,128)} %bitcast.9, f32[2,32,128]{2,1,0:T(8,128)} %get-tuple-element.7.sep_ref, bf16[2,512,256]{2,1,0:T(8,128)(2,1)} %get-tuple-element.8.gath_ref, f32[2,256,128]{2,1,0:T(8,128)} %get-tuple-element.9.coord_ref), custom_call_target="tpu_custom_call" | custom-call | tf_op jit(solution)/shard_map/last/pallas_call | solution.py:443

commit v5 on v4

--- a/solution.py
+++ b/solution.py
@@ -376,8 +376,8 @@
         (mm1, 0, 0), (mm1, 0, 1), (mm1, 0, 2), (mm1, 0, 3), (ar1, 0), (ar2, 0), (step5, 1),
         (mm1, 1, 0), (mm1, 1, 1), (mm1, 1, 2), (mm1, 1, 3), (ar1, 1), (ar2, 1), (ar3, 0),
         (settle,), (ar4, 0), (ar3, 1), (ar5, 0), (rs1, 0), (ar4, 1), (ar5, 1), (rs1, 1), (settle,), (rs3, 0),
-        (rs5, 0), (top_z, 0), (rs6, 0), (rs3, 1), (top_plane, 0), (mode_send, 0), (rs5, 1), (top_z, 1), (rs6, 1),
-        (settle,), (top_plane, 1), (top_core, 0), (mode_send, 1), (separators, 0), (settle,), (top_core, 1), (gather_top, 0),
+        (rs5, 0), (top_z, 0), (rs6, 0), (rs3, 1), (top_plane, 0), (rs5, 1), (top_z, 1), (rs6, 1),
+        (settle,), (top_plane, 1), (top_core, 0), (mode_send, 0), (mode_send, 1), (separators, 0), (settle,), (top_core, 1), (gather_top, 0),
         (separators, 1), (gather_top, 1), (settle,), (gather_sep, 0), (mode_recv, 0), (mode_recv, 1), (settle,), (gather_sep, 1),
     ]
     for step, *args in program[:STOP] + [(sent,)]:

time: 85.5 us -> 86.2 us (level)
  no operation moved by 1% of the time
where the time goes in v5:
time: 86.2 us; the launch traced here: 86.1 us
  Pallas kernels  85.5 us (99%)
    pallas_call x1, Pallas kernels, on_device(): pl.pallas_call(kernel, out_shape=(jax.ShapeDtypeStruct((NH, 32, 128), F32...  79.1 us
    pallas_call x1, Pallas kernels, on_device(): pl.pallas_call(last, grid=(2,), out_shape=(jax.ShapeDtypeStruct((32, 256)...  6.32 us

profile of v5, /device:TPU:1, one launch (start us, length us, event | category | flops | bytes accessed | tf_op | source)
XLA Modules:
  0.0 86.1 jit_solution(7343083719693622395)
XLA Ops:
  0.6 79.1 %step.1 = (f32[2,32,128]{2,1,0:T(8,128)}, bf16[2,512,256]{2,1,0:T(8,128)(2,1)}, f32[2,256,128]{2,1,0:T(8,128)}) custom-call(f32[2048,1024]{1,0:T(8,128)} %op_hbm.1, f32[16,2048]{1,0:T(8,128)} %bitcast.11, s32[1,88]{1,0:T(1,128)} %bitcast.15, f32[32,1024]{1,0:T(8,128)} %bitcast.12, s32[1,512]{1,0:T(1,128)} %bitcast.14), custom_call_target="tpu_custom_call" | custom-call | flops 8999999488 | bytes 20000000 | tf_op jit(solution)/shard_map/step/pallas_call | solution.py:421
  79.8 6.3 %last.1 = (f32[32,256]{1,0:T(8,128)}, f32[2048,256]{1,0:T(8,128)}) custom-call(f32[2048,512]{1,0:T(8,128)} %bitcast.8, f32[2048,256]{1,0:T(8,128)} %bitcast.9, f32[2,32,128]{2,1,0:T(8,128)} %get-tuple-element.7.sep_ref, bf16[2,512,256]{2,1,0:T(8,128)(2,1)} %get-tuple-element.8.gath_ref, f32[2,256,128]{2,1,0:T(8,128)} %get-tuple-element.9.coord_ref), custom_call_target="tpu_custom_call" | custom-call | tf_op jit(solution)/shard_map/last/pallas_call | solution.py:443

commit v6 on v4

--- a/solution.py
+++ b/solution.py
@@ -370,8 +370,8 @@
             c.wait()
 
     program = [
-        (own_sends, 0), (own_sends, 1), (select_modes,), (select_ancestors,), (split_coupling,),
-        (step2, 0), (step3, 0), (split_k, 0), (split_k, 1), (split_k, 2), (split_k, 3), (step2, 1), (step3, 1),
+        (own_sends, 0), (select_modes,), (select_ancestors,), (split_coupling,),
+        (step2, 0), (own_sends, 1), (step3, 0), (split_k, 0), (split_k, 1), (split_k, 2), (split_k, 3), (step2, 1), (step3, 1),
         (split_k, 4), (split_k, 5), (split_k, 6), (split_k, 7), (step4, 0), (step4, 1), (step5, 0),
         (mm1, 0, 0), (mm1, 0, 1), (mm1, 0, 2), (mm1, 0, 3), (ar1, 0), (ar2, 0), (step5, 1),
         (mm1, 1, 0), (mm1, 1, 1), (mm1, 1, 2), (mm1, 1, 3), (ar1, 1), (ar2, 1), (ar3, 0),

time: 85.5 us -> 88.1 us (1.030)
  Pallas kernels: 84.8 us -> 87.3 us
    pallas_call x1, Pallas kernels: 78.5 us -> 81 us  [on_device(): pl.pallas_call(kernel, out_shape=(jax.ShapeDtypeStruct((NH, 32, 128), F32...]
where the time goes in v6:
time: 88.1 us; the launch traced here: 88 us
  Pallas kernels  87.3 us (99%)
    pallas_call x1, Pallas kernels, on_device(): pl.pallas_call(kernel, out_shape=(jax.ShapeDtypeStruct((NH, 32, 128), F32...  81 us
    pallas_call x1, Pallas kernels, on_device(): pl.pallas_call(last, grid=(2,), out_shape=(jax.ShapeDtypeStruct((32, 256)...  6.32 us

profile of v6, /device:TPU:1, one launch (start us, length us, event | category | flops | bytes accessed | tf_op | source)
XLA Modules:
  0.0 88.0 jit_solution(6753991104034162167)
XLA Ops:
  0.6 81.0 %step.1 = (f32[2,32,128]{2,1,0:T(8,128)}, bf16[2,512,256]{2,1,0:T(8,128)(2,1)}, f32[2,256,128]{2,1,0:T(8,128)}) custom-call(f32[2048,1024]{1,0:T(8,128)} %op_hbm.1, f32[16,2048]{1,0:T(8,128)} %bitcast.11, s32[1,88]{1,0:T(1,128)} %bitcast.15, f32[32,1024]{1,0:T(8,128)} %bitcast.12, s32[1,512]{1,0:T(1,128)} %bitcast.14), custom_call_target="tpu_custom_call" | custom-call | flops 8999999488 | bytes 20000000 | tf_op jit(solution)/shard_map/step/pallas_call | solution.py:421
  81.6 6.3 %last.1 = (f32[32,256]{1,0:T(8,128)}, f32[2048,256]{1,0:T(8,128)}) custom-call(f32[2048,512]{1,0:T(8,128)} %bitcast.8, f32[2048,256]{1,0:T(8,128)} %bitcast.9, f32[2,32,128]{2,1,0:T(8,128)} %get-tuple-element.7.sep_ref, bf16[2,512,256]{2,1,0:T(8,128)(2,1)} %get-tuple-element.8.gath_ref, f32[2,256,128]{2,1,0:T(8,128)} %get-tuple-element.9.coord_ref), custom_call_target="tpu_custom_call" | custom-call | tf_op jit(solution)/shard_map/last/pallas_call | solution.py:443
